TPU v7x, 512 devices: a whole 4x4x16 slice. The times are simulated.
512 devices in a mesh: vocab: 16 (over z), rows: 32 (over y, x, core).
Axes of the slice: x: 4, y: 4, z: 16, core: 2. Of those that a mesh axis runs over, the one named last changes fastest.
Arguments:
- trunk_hidden: bfloat16 [128, 7168], P('rows'), may hold values from -8 to 8
- mtp_state: bfloat16 [128, 7168], P('rows'), may hold values from -24 to 24, as said below
- mtp_gain: bfloat16 [7168], replicated, may hold values from 0.099609375 to 1.8984375
- head_weight: bfloat16 [73728, 7168], P(('vocab', 'rows')), may hold values from -0.28347335 to 0.28347335, as said below
- target_ids: int32 [128], replicated, may hold values from 0 to 73727
- mtp_target_ids: int32 [128], replicated, may hold values from 0 to 73727
- attn_values: bfloat16 [128, 64, 128], P('rows'), may hold values from -6 to 6
- out_proj: bfloat16 [8192, 7168], P('rows', 'vocab'), may hold values from -0.0625 to 0.0625
Outputs:
- grad_trunk: bfloat16 [128, 7168], P('rows')
- grad_residual: bfloat16 [128, 7168], P('rows')
- grad_gain: float32 [7168], replicated
- grad_head: bfloat16 [73728, 7168], P(('vocab', 'rows'))
- grad_attn: bfloat16 [128, 64, 128], P('vocab', 'rows')
- grad_out_proj: bfloat16 [8192, 7168], P('rows', 'vocab')
Inputs may be any that keep to these rules, and one draw needn't show every extreme that they name: `mtp_state`: block outputs; rows differ in scale. `head_weight`: head rows.
All inputs are finite; a program needn't handle non-finite values.
Results may differ from a plain program's by a relative error of at most 0.025.
Values may be sent and summed in bfloat16 or wider, within the bound.
A program may use at most 64 MiB of HBM per device.

v0:
```python
import jax
import jax.numpy as jnp
from jax import lax
from jax.sharding import PartitionSpec as P

loss_scale = 8.0
mtp_share = 0.3
norm_eps = 1e-06


def normalize(state):
    values = state.astype(jnp.float32)
    inverse = lax.rsqrt(jnp.mean(values * values, axis=-1, keepdims=True) + norm_eps)
    return (values * inverse, inverse)


def local(
    trunk_hidden,
    mtp_state,
    mtp_gain,
    head_weight,
    target_ids,
    mtp_target_ids,
    attn_values,
    out_proj,
):
    tok_local = trunk_hidden.shape[0]
    row_count = lax.axis_size("rows")
    vocab_rows = head_weight.shape[0]
    gain = mtp_gain.astype(jnp.float32)
    normed, inverse = normalize(mtp_state)
    mtp_hidden = (normed * gain).astype(jnp.bfloat16)
    stacked = jnp.concatenate([trunk_hidden, mtp_hidden], axis=0)
    targets = jnp.stack(
        [target_ids.reshape(row_count, tok_local), mtp_target_ids.reshape(row_count, tok_local)],
        axis=1,
    ).reshape(-1)
    shares = jnp.stack(
        [
            jnp.full((row_count, tok_local), loss_scale, jnp.float32),
            jnp.full((row_count, tok_local), loss_scale * mtp_share, jnp.float32),
        ],
        axis=1,
    ).reshape(-1)
    block_index = lax.axis_index("vocab") * row_count + lax.axis_index("rows")
    vocab_ids = block_index * vocab_rows + jnp.arange(vocab_rows, dtype=jnp.int32)
    onehot = (targets[:, None] == vocab_ids[None, :]).astype(jnp.float32)
    gathered = lax.all_gather(stacked, "rows", axis=0, tiled=True)
    logits = lax.dot_general(
        gathered, head_weight, (((1,), (1,)), ((), ())), preferred_element_type=jnp.float32
    )
    local_max = jnp.max(logits, axis=1)
    top = lax.pmax(local_max, ("vocab", "rows"))
    total = lax.psum(jnp.sum(jnp.exp(logits - top[:, None]), axis=1), ("vocab", "rows"))
    logit_grads = (
        shares[:, None] * (jnp.exp(logits - top[:, None]) / total[:, None] - onehot)
    ).astype(jnp.bfloat16)
    feature_width = out_proj.shape[1]
    column_start = lax.axis_index("vocab") * feature_width
    own_terms = lax.psum_scatter(
        jnp.dot(logit_grads, head_weight, preferred_element_type=jnp.float32).astype(jnp.bfloat16),
        "rows",
        scatter_dimension=0,
        tiled=True,
    )
    grad_hidden = lax.psum(own_terms, "vocab").astype(jnp.float32)
    head_total = lax.dot_general(
        logit_grads, gathered, (((0,), (0,)), ((), ())), preferred_element_type=jnp.float32
    )
    grad_head = head_total.astype(jnp.bfloat16)
    grad_trunk = grad_hidden[:tok_local].astype(jnp.bfloat16)
    mtp_grad = grad_hidden[tok_local:]
    grad_gain = lax.psum(jnp.sum(mtp_grad * normed, axis=0), "rows")
    scaled = mtp_grad * gain
    dot_mean = jnp.mean(scaled * normed, axis=-1, keepdims=True)
    grad_residual = (inverse * (scaled - normed * dot_mean)).astype(jnp.bfloat16)
    own_columns = lax.dynamic_slice_in_dim(grad_residual, column_start, feature_width, 1)
    all_columns = lax.all_gather(own_columns, "rows", axis=0, tiled=True)
    partial_attn = lax.dot_general(
        all_columns, out_proj, (((1,), (1,)), ((), ())), preferred_element_type=jnp.float32
    )
    attn_share = lax.psum_scatter(
        partial_attn.astype(jnp.bfloat16), "vocab", scatter_dimension=0, tiled=True
    ).astype(jnp.float32)
    head_count = out_proj.shape[0] // attn_values.shape[2]
    grad_attn = attn_share.astype(jnp.bfloat16).reshape(
        attn_share.shape[0], head_count, attn_values.shape[2]
    )
    proj_grads = jnp.einsum(
        "tkh,td->khd",
        lax.all_to_all(attn_values, "rows", split_axis=1, concat_axis=0, tiled=True),
        all_columns,
        preferred_element_type=jnp.float32,
    ).astype(jnp.bfloat16)
    grad_out_proj = proj_grads.reshape(out_proj.shape[0], feature_width)
    return (grad_trunk, grad_residual, grad_gain, grad_head, grad_attn, grad_out_proj)


def solution(mesh):
    return jax.shard_map(
        local,
        mesh=mesh,
        in_specs=(
            P("rows", None),
            P("rows", None),
            P(),
            P(("vocab", "rows"), None),
            P(),
            P(),
            P("rows", None, None),
            P("rows", "vocab"),
        ),
        out_specs=(
            P("rows", None),
            P("rows", None),
            P(),
            P(("vocab", "rows"), None),
            P("vocab", "rows", None),
            P("rows", "vocab"),
        ),
        check_vma=False,
    )
```

profile of v0, /device:TPU:32, one launch (start us, length us, event | category | flops | bytes accessed | tf_op | source)
XLA Modules:
  0.0 686.7 jit_solution(3278536386553361159)
XLA Ops:
  7.2 0.0 copy-start
  7.2 0.0 copy-start.5
  7.2 0.0 all-gather.3.cloned.1.call-start
  7.2 1.1 fusion.11
  8.4 0.7 convert_element_type.38
  9.1 0.9 fusion.9
  10.0 1.5 pad_maximum_fusion
  11.5 0.0 all-gather.3.cloned.1.call-update
  11.6 0.0 reduce-scatter.3.cloned.1.call-start
  11.6 0.8 stack_reshape.6
  12.4 0.8 stack_reshape.7
  13.2 0.1 eq.15
  13.3 63.5 %all-gather.3.cloned.1.call-done = bf16[256,7168]{1,0:T(8,128)(2,1)} async-done(((bf16[8,7168]{1,0:T(8,128)(2,1)}), bf16[256,7168]{1,0:T(8,128)(2,1)}) %all-gather.3.cloned.1.call-update) | async-done | bytes 3670032 | tf_op jit(solution)/shard_map/all_gather | solution.py:48
  76.8 0.0 copy-done
  76.8 3.4 fusion.13
  80.2 102.8 %pmax.7 = f32[256]{0:T(256)S(1)} all-reduce(f32[256]{0:T(256)S(1)} %get-tuple-element.32), channel_id=1, replica_groups=mesh['vocab'=16,'rows'=32] {'vocab','rows'}, use_global_device_ids=true, to_apply=%region_2.0 | all-reduce | flops 256 | bytes 2048 | tf_op jit(solution)/shard_map/pmax | solution.py:53
  183.0 101.3 %psum.21 = f32[256]{0:T(256)S(1)} all-reduce(f32[256]{0:T(256)S(1)} %fusion.5), channel_id=1, replica_groups=mesh['vocab'=16,'rows'=32] {'vocab','rows'}, use_global_device_ids=true, to_apply=%region_4.0 | all-reduce | flops 256 | bytes 2048 | tf_op jit(solution)/shard_map/psum | solution.py:54
  284.3 0.0 copy-done.5
  284.3 0.0 copy-start.4
  284.3 3.1 convolution_convert_fusion
  287.4 0.0 reduce-scatter.3.cloned.1.call-update
  287.4 0.0 copy-done.4
  287.4 0.0 copy-start.1
  287.4 0.0 copy-start.2
  287.5 0.7 copy.30
  288.1 4.3 all-to-all-start
  292.4 0.0 all-reduce.2.cloned.1.call-start
  292.5 7.4 %all-to-all-done = bf16[4,64,128]{2,0,1:T(4,128)(2,1)S(1)} async-done(((bf16[4,64,128]{2,0,1:T(4,128)(2,1)}), bf16[4,64,128]{2,0,1:T(4,128)(2,1)S(1)}, u32[]{:S(2)}, u32[]{:S(2)}) %all-to-all-start) | async-done | bytes 65568 | tf_op jit(solution)/shard_map/all_to_all | solution.py:91
  300.0 86.5 %reduce-scatter.3.cloned.1.call-done = bf16[8,7168]{1,0:T(8,128)(2,1)} async-done(((bf16[256,7168]{1,0:T(8,128)(2,1)}), bf16[8,7168]{1,0:T(8,128)(2,1)}) %reduce-scatter.3.cloned.1.call-update) | async-done | bytes 114704 | tf_op jit(solution)/shard_map/reduce_scatter | solution.py:60
  386.4 0.0 all-reduce.2.cloned.1.call-update
  386.4 0.0 reduce-scatter.5.cloned.1.call-start
  386.5 4.1 convolution_convert_fusion.1
  390.6 131.7 %all-reduce.2.cloned.1.call-done = bf16[8,7168]{1,0:T(8,128)(2,1)} async-done(((bf16[8,7168]{1,0:T(8,128)(2,1)}), bf16[8,7168]{1,0:T(8,128)(2,1)}) %all-reduce.2.cloned.1.call-update) | async-done | bytes 114704 | tf_op jit(solution)/shard_map/psum | solution.py:66
  522.3 0.0 copy-done.1
  522.3 1.2 fusion.12
  523.5 1.0 fusion.8
  524.5 0.0 copy-start.3
  524.5 0.1 dynamic-slice_bitcast_fusion
  524.6 24.6 %all-gather = bf16[32,4,448]{2,1,0:T(4,128)(2,1)S(1)} all-gather(bf16[1,4,448]{2,1,0:T(4,128)(2,1)S(1)} %dynamic-slice_bitcast_fusion), channel_id=1, replica_groups=mesh['vocab'=16,'rows'=32] {'rows'}, dimensions={0}, use_global_device_ids=true | all-gather | bytes 118272 | tf_op jit(solution)/shard_map/all_gather | solution.py:78
  549.2 0.1 reshape.41
  549.2 0.0 copy-done.2
  549.2 0.8 convolution_convert_fusion.3
  550.1 0.0 reduce-scatter.5.cloned.1.call-update
  550.1 0.2 fusion
  550.3 0.7 copy.39
  551.1 1.5 slice.13
  552.6 126.3 %psum.23 = f32[7168]{0:T(1024)} all-reduce(f32[7168]{0:T(1024)S(1)} %get-tuple-element.30), channel_id=1, replica_groups=mesh['vocab'=16,'rows'=32] {'rows'}, use_global_device_ids=true, to_apply=%region_9.0 | all-reduce | flops 7168 | bytes 57344 | tf_op jit(solution)/shard_map/psum | solution.py:73
  678.9 0.0 reduce-scatter.5.cloned.1.call-done
  678.9 1.3 copy.34
  680.2 0.0 copy-done.3
  (7 shorter events, 0.1 us)
Async XLA Ops:
  7.2 69.6 %copy-start = (bf16[144,7168]{1,0:T(8,128)(2,1)S(1)}, bf16[144,7168]{1,0:T(8,128)(2,1)}, u32[]{:S(2)}) copy-start(bf16[144,7168]{1,0:T(8,128)(2,1)} %param.11) | copy-start | bytes 6193156
  7.2 277.2 %copy-start.5 = (f32[256]{0:T(256)S(1)}, f32[256]{0:T(256)}, u32[]{:S(2)}) copy-start(f32[256]{0:T(256)} %constant.6.clone.1) | copy-start | bytes 3076
  7.2 69.6 %all-gather.3.cloned.1.call-start = ((), (), s32[]{:S(2)}) async-start(), calls=%async_computation.3 | async-start | bytes 3784704 | tf_op jit(solution)/shard_map/all_gather | solution.py:48
  11.6 374.8 %reduce-scatter.3.cloned.1.call-start = ((), (), s32[]{:S(2)}) async-start(), calls=%async_computation.4 | async-start | bytes 3784704 | tf_op jit(solution)/shard_map/reduce_scatter | solution.py:60
  284.3 3.1 copy-start.4
  287.4 234.9 %copy-start.1 = (bf16[4,7168]{1,0:T(4,128)(2,1)S(1)}, bf16[4,7168]{1,0:T(4,128)(2,1)}, u32[]{:S(2)}) copy-start(bf16[4,7168]{1,0:T(4,128)(2,1)} %param.9) | copy-start | bytes 172036
  287.4 261.8 %copy-start.2 = (bf16[256,448]{0,1:T(8,128)(2,1)S(1)}, bf16[256,448]{0,1:T(8,128)(2,1)}, u32[]{:S(2)}) copy-start(bf16[256,448]{0,1:T(8,128)(2,1)} %param.15) | copy-start | bytes 688132
  288.1 11.8 %all-to-all-start = ((bf16[4,64,128]{2,0,1:T(4,128)(2,1)}), bf16[4,64,128]{2,0,1:T(4,128)(2,1)S(1)}, u32[]{:S(2)}, u32[]{:S(2)}) async-start(bf16[4,64,128]{2,0,1:T(4,128)(2,1)} %copy.30), calls=%async_computation.2 | async-start | bytes 131072 | tf_op jit(solution)/shard_map/all_to_all | solution.py:91
  292.4 229.8 %all-reduce.2.cloned.1.call-start = ((), (), s32[]{:S(2)}) async-start(), calls=%async_computation.5 | async-start | bytes 229376 | tf_op jit(solution)/shard_map/psum | solution.py:66
  386.4 292.5 %reduce-scatter.5.cloned.1.call-start = ((), (), s32[]{:S(2)}) async-start(), calls=%async_computation.6 | async-start | bytes 69632 | tf_op jit(solution)/shard_map/reduce_scatter | solution.py:82
  524.5 155.7 %copy-start.3 = (bf16[4,7168]{1,0:T(4,128)(2,1)}, bf16[4,7168]{1,0:T(4,128)(2,1)S(1)}, u32[]{:S(2)}) copy-start(bf16[4,7168]{1,0:T(4,128)(2,1)S(1)} %fusion.8) | copy-start | bytes 172036
Sparse Core Ops, SparseCore 0:
  11.7 65.0 all-gather.2
  287.5 98.8 reduce-scatter.2
  388.9 133.3 all-reduce.1
  550.2 62.4 reduce-scatter.4
where the time goes:
time: 687 us
  blocking collectives  355 us (52%)
  waiting for transfers between devices  289 us (42%)
  between operations  13.9 us (2%)
  matrix products  11.6 us (2%)
    psum x1, waiting for transfers between devices, local(): grad_hidden = lax.psum(own_terms, 'vocab').astype(jnp.float32)  132 us
    psum x1, blocking collectives, local(): grad_gain = lax.psum(jnp.sum(mtp_grad * normed, axis=0), 'rows')  126 us
    pmax x1, blocking collectives, local(): top = lax.pmax(local_max, ('vocab', 'rows'))  103 us
    psum x1, blocking collectives, local(): lax.psum(jnp.sum(jnp.exp(logits - top[:, None]), axis=1), ('vocab', 'rows'))  101 us
    reduce_scatter x1, waiting for transfers between devices, local(): lax.psum_scatter(jnp.dot(logit_grads, head_weight, preferred_element_type...  86.5 us
    all_gather x1, waiting for transfers between devices, local(): gathered = lax.all_gather(stacked, 'rows', axis=0, tiled=True)  63.5 us
    all_gather x1, blocking collectives, local(): all_columns = lax.all_gather(own_columns, 'rows', axis=0, tiled=True)  24.6 us
  transfers between devices with their start and end apart: 5, of which 4 were waited for; matrix products, arithmetic and copies ran while one was open for 1% of the time, Pallas kernels for 0%

commit v1 on v0

--- a/solution.py
+++ b/solution.py
@@ -51,7 +51,9 @@
     )
     local_max = jnp.max(logits, axis=1)
     top = lax.pmax(local_max, ("vocab", "rows"))
-    total = lax.psum(jnp.sum(jnp.exp(logits - top[:, None]), axis=1), ("vocab", "rows"))
+    total = jnp.sum(
+        lax.all_gather(jnp.sum(jnp.exp(logits - top[:, None]), axis=1), ("vocab", "rows")), axis=0
+    )
     logit_grads = (
         shares[:, None] * (jnp.exp(logits - top[:, None]) / total[:, None] - onehot)
     ).astype(jnp.bfloat16)

time: 687 us -> 701 us (1.020)
  blocking collectives: 355 us -> 367 us
    all_gather x0 -> x1, blocking collectives: none -> 113 us  [local(): lax.all_gather(jnp.sum(jnp.exp(logits - top[:, None]), axis=1), ('vocab',...]
    psum x1 -> x0, blocking collectives: 101 us -> none  [local(): lax.psum(jnp.sum(jnp.exp(logits - top[:, None]), axis=1), ('vocab', 'rows'))]
where the time goes in v1:
time: 701 us; the launch traced here: 700 us
  blocking collectives  367 us (52%)
  waiting for transfers between devices  290 us (41%)
  between operations  13.9 us (2%)
  matrix products  11.6 us (2%)
  other arithmetic  7.15 us (1%)
    psum x1, waiting for transfers between devices, local(): grad_hidden = lax.psum(own_terms, 'vocab').astype(jnp.float32)  132 us
    psum x1, blocking collectives, local(): grad_gain = lax.psum(jnp.sum(mtp_grad * normed, axis=0), 'rows')  126 us
    all_gather x1, blocking collectives, local(): lax.all_gather(jnp.sum(jnp.exp(logits - top[:, None]), axis=1), ('vocab',...  113 us
    pmax x1, blocking collectives, local(): top = lax.pmax(local_max, ('vocab', 'rows'))  103 us
    reduce_scatter x1, waiting for transfers between devices, local(): lax.psum_scatter(jnp.dot(logit_grads, head_weight, preferred_element_type...  87.6 us
    all_gather x1, waiting for transfers between devices, local(): gathered = lax.all_gather(stacked, 'rows', axis=0, tiled=True)  63.4 us
    all_gather x1, blocking collectives, local(): all_columns = lax.all_gather(own_columns, 'rows', axis=0, tiled=True)  24.6 us
  transfers between devices with their start and end apart: 5, of which 4 were waited for; matrix products, arithmetic and copies ran while one was open for 1% of the time, Pallas kernels for 0%

profile of v1, /device:TPU:32, one launch (start us, length us, event | category | flops | bytes accessed | tf_op | source)
XLA Modules:
  0.0 700.4 jit_solution(15182781456410805347)
XLA Ops:
  7.2 0.0 copy-start
  7.2 0.0 all-gather.5.cloned.1.call-start
  7.2 1.1 fusion.11
  8.4 0.7 convert_element_type.38
  9.1 0.9 fusion.9
  10.0 1.5 pad_maximum_fusion
  11.5 0.0 all-gather.5.cloned.1.call-update
  11.6 0.0 copy-start.5
  11.6 0.0 reduce-scatter.3.cloned.1.call-start
  11.6 0.8 stack_reshape.6
  12.4 0.8 stack_reshape.7
  13.2 0.1 eq.15
  13.3 63.4 %all-gather.5.cloned.1.call-done = bf16[256,7168]{1,0:T(8,128)(2,1)} async-done(((bf16[8,7168]{1,0:T(8,128)(2,1)}), bf16[256,7168]{1,0:T(8,128)(2,1)}) %all-gather.5.cloned.1.call-update) | async-done | bytes 3670032 | tf_op jit(solution)/shard_map/all_gather | solution.py:48
  76.8 0.0 copy-done
  76.8 3.4 fusion.13
  80.2 102.8 %pmax.7 = f32[256]{0:T(256)S(1)} all-reduce(f32[256]{0:T(256)S(1)} %get-tuple-element.32), channel_id=1, replica_groups=mesh['vocab'=16,'rows'=32] {'vocab','rows'}, use_global_device_ids=true, to_apply=%region_2.0 | all-reduce | flops 256 | bytes 2048 | tf_op jit(solution)/shard_map/pmax | solution.py:53
  183.0 113.2 %all-gather.1 = f32[512,1,256]{2,1,0:T(1,128)S(1)} all-gather(f32[1,1,256]{2,1,0:T(1,128)S(1)} %bitcast.27), channel_id=2, replica_groups=mesh['vocab'=16,'rows'=32] {'vocab','rows'}, dimensions={0}, use_global_device_ids=true | all-gather | bytes 525312 | tf_op jit(solution)/shard_map/all_gather | solution.py:55
  296.3 0.6 reduce_sum.47
  296.8 0.0 copy-done.5
  296.8 0.0 copy-start.4
  296.8 3.1 convolution_convert_fusion
  299.9 0.0 reduce-scatter.3.cloned.1.call-update
  299.9 0.0 copy-done.4
  299.9 0.0 copy-start.1
  299.9 0.0 copy-start.2
  299.9 0.7 copy.30
  300.6 4.3 all-to-all-start
  305.0 0.0 all-reduce.2.cloned.1.call-start
  305.0 7.4 %all-to-all-done = bf16[4,64,128]{2,0,1:T(4,128)(2,1)S(1)} async-done(((bf16[4,64,128]{2,0,1:T(4,128)(2,1)}), bf16[4,64,128]{2,0,1:T(4,128)(2,1)S(1)}, u32[]{:S(2)}, u32[]{:S(2)}) %all-to-all-start) | async-done | bytes 65568 | tf_op jit(solution)/shard_map/all_to_all | solution.py:93
  312.5 87.6 %reduce-scatter.3.cloned.1.call-done = bf16[8,7168]{1,0:T(8,128)(2,1)} async-done(((bf16[256,7168]{1,0:T(8,128)(2,1)}), bf16[8,7168]{1,0:T(8,128)(2,1)}) %reduce-scatter.3.cloned.1.call-update) | async-done | bytes 114704 | tf_op jit(solution)/shard_map/reduce_scatter | solution.py:62
  400.0 0.0 all-reduce.2.cloned.1.call-update
  400.1 0.0 reduce-scatter.5.cloned.1.call-start
  400.1 4.1 convolution_convert_fusion.1
  404.2 131.7 %all-reduce.2.cloned.1.call-done = bf16[8,7168]{1,0:T(8,128)(2,1)} async-done(((bf16[8,7168]{1,0:T(8,128)(2,1)}), bf16[8,7168]{1,0:T(8,128)(2,1)}) %all-reduce.2.cloned.1.call-update) | async-done | bytes 114704 | tf_op jit(solution)/shard_map/psum | solution.py:68
  535.9 0.0 copy-done.1
  535.9 1.2 fusion.12
  537.1 1.0 fusion.8
  538.2 0.0 copy-start.3
  538.2 0.1 dynamic-slice_bitcast_fusion
  538.3 24.6 %all-gather.2 = bf16[32,4,448]{2,1,0:T(4,128)(2,1)S(1)} all-gather(bf16[1,4,448]{2,1,0:T(4,128)(2,1)S(1)} %dynamic-slice_bitcast_fusion), channel_id=1, replica_groups=mesh['vocab'=16,'rows'=32] {'rows'}, dimensions={0}, use_global_device_ids=true | all-gather | bytes 118272 | tf_op jit(solution)/shard_map/all_gather | solution.py:80
  562.8 0.1 reshape.44
  562.9 0.0 copy-done.2
  562.9 0.8 convolution_convert_fusion.3
  563.7 0.0 reduce-scatter.5.cloned.1.call-update
  563.7 0.2 fusion
  564.0 0.7 copy.39
  564.7 1.5 slice.13
  566.2 126.3 %psum.15 = f32[7168]{0:T(1024)} all-reduce(f32[7168]{0:T(1024)S(1)} %get-tuple-element.30), channel_id=1, replica_groups=mesh['vocab'=16,'rows'=32] {'rows'}, use_global_device_ids=true, to_apply=%region_9.0 | all-reduce | flops 7168 | bytes 57344 | tf_op jit(solution)/shard_map/psum | solution.py:75
  692.6 0.0 reduce-scatter.5.cloned.1.call-done
  692.6 1.3 copy.34
  693.9 0.0 copy-done.3
  (7 shorter events, 0.1 us)
Async XLA Ops:
  7.2 69.6 %copy-start = (bf16[144,7168]{1,0:T(8,128)(2,1)S(1)}, bf16[144,7168]{1,0:T(8,128)(2,1)}, u32[]{:S(2)}) copy-start(bf16[144,7168]{1,0:T(8,128)(2,1)} %param.11) | copy-start | bytes 6193156
  7.2 69.6 %all-gather.5.cloned.1.call-start = ((), (), s32[]{:S(2)}) async-start(), calls=%async_computation.3 | async-start | bytes 3784704 | tf_op jit(solution)/shard_map/all_gather | solution.py:48
  11.6 285.3 %copy-start.5 = (f32[256]{0:T(256)S(1)}, f32[256]{0:T(256)}, u32[]{:S(2)}) copy-start(f32[256]{0:T(256)} %constant.6.clone.1) | copy-start | bytes 3076
  11.6 388.5 %reduce-scatter.3.cloned.1.call-start = ((), (), s32[]{:S(2)}) async-start(), calls=%async_computation.4 | async-start | bytes 3784704 | tf_op jit(solution)/shard_map/reduce_scatter | solution.py:62
  296.8 3.1 copy-start.4
  299.9 236.0 %copy-start.1 = (bf16[4,7168]{1,0:T(4,128)(2,1)S(1)}, bf16[4,7168]{1,0:T(4,128)(2,1)}, u32[]{:S(2)}) copy-start(bf16[4,7168]{1,0:T(4,128)(2,1)} %param.9) | copy-start | bytes 172036
  299.9 263.0 %copy-start.2 = (bf16[256,448]{0,1:T(8,128)(2,1)S(1)}, bf16[256,448]{0,1:T(8,128)(2,1)}, u32[]{:S(2)}) copy-start(bf16[256,448]{0,1:T(8,128)(2,1)} %param.15) | copy-start | bytes 688132
  300.6 11.8 %all-to-all-start = ((bf16[4,64,128]{2,0,1:T(4,128)(2,1)}), bf16[4,64,128]{2,0,1:T(4,128)(2,1)S(1)}, u32[]{:S(2)}, u32[]{:S(2)}) async-start(bf16[4,64,128]{2,0,1:T(4,128)(2,1)} %copy.30), calls=%async_computation.2 | async-start | bytes 131072 | tf_op jit(solution)/shard_map/all_to_all | solution.py:93
  305.0 231.0 %all-reduce.2.cloned.1.call-start = ((), (), s32[]{:S(2)}) async-start(), calls=%async_computation.5 | async-start | bytes 229376 | tf_op jit(solution)/shard_map/psum | solution.py:68
  400.1 292.5 %reduce-scatter.5.cloned.1.call-start = ((), (), s32[]{:S(2)}) async-start(), calls=%async_computation.6 | async-start | bytes 69632 | tf_op jit(solution)/shard_map/reduce_scatter | solution.py:84
  538.2 155.7 %copy-start.3 = (bf16[4,7168]{1,0:T(4,128)(2,1)}, bf16[4,7168]{1,0:T(4,128)(2,1)S(1)}, u32[]{:S(2)}) copy-start(bf16[4,7168]{1,0:T(4,128)(2,1)S(1)} %fusion.8) | copy-start | bytes 172036
Sparse Core Ops, SparseCore 0:
  11.7 65.0 all-gather.4
  300.0 99.9 reduce-scatter.2
  402.5 133.3 all-reduce.1
  563.9 62.4 reduce-scatter.4
